TPU v7x, 32 devices: a whole 2x2x4 slice. The times are simulated.
32 devices in a mesh: parts: 2 (over y), expert: 4 (over z), dp: 2 (over x), tensor: 2 (over core).
Axes of the slice: x: 2, y: 2, z: 4, core: 2. Of those that a mesh axis runs over, the one named last changes fastest.
Arguments:
- tokens: bfloat16 [4096, 7168], P(('parts', 'expert', 'tensor'), 'dp'), parts along dimension 0, may hold values from -6 to 6
- cotangent: bfloat16 [4096, 7168], P(('parts', 'expert', 'tensor'), 'dp'), parts along dimension 0, may hold values from -0.59765625 to 0.59765625
- norm_gain: float32 [7168], P('dp'), may hold values from 0.5 to 1.5
- expert_ids: int32 [4096, 1], P(('parts', 'expert', 'tensor')), parts along dimension 0, may hold values from 0 to 1; in each aligned block of 256 rows (0 to 255, 256 to 511, ...) at most 160 rows name the same one
- combine_weight: float32 [4096], P(('parts', 'expert', 'tensor')), parts along dimension 0, may hold values from 0.2 to 1
- up_weight: bfloat16 [7168, 2048], P('dp', ('expert', 'tensor')), may hold values from -0.0625 to 0.0625
- down_weight: bfloat16 [2048, 7168], P(('expert', 'tensor'), 'dp'), may hold values from -0.1875 to 0.1875
Outputs:
- token_grad: bfloat16 [4096, 7168], P(('parts', 'expert', 'tensor'), 'dp'), parts along dimension 0
- up_grad: bfloat16 [14336, 2048], P(('parts', 'dp'), ('expert', 'tensor')), parts along dimension 0
- down_grad: bfloat16 [4096, 7168], P(('parts', 'expert', 'tensor'), 'dp'), parts along dimension 0
- gain_grad: float32 [14336], P(('parts', 'dp')), parts along dimension 0
- token_inner: float32 [4096], P(('parts', 'expert', 'tensor')), parts along dimension 0
There are 2 independent parts, one for each index of `parts`. A program takes and returns all parts, laid end to end along the dimension named above; an argument that names none is the same for every part. Nothing has to cross between parts.
Inputs may be any that keep to these rules, and one draw needn't show every extreme that they name: `expert_ids`: each row names one routed expert. Within the rows of one device (aligned blocks of 256 rows) no expert is named by more than 160 rows, a bound that some block reaches.
All inputs are finite; a program needn't handle non-finite values.
Results may differ from a plain program's by a relative error of at most 0.014.
Values may be sent and summed in bfloat16 or wider, within the bound.
A program may use at most 128 MiB of HBM per device.

v0:
```python
import jax
import jax.numpy as jnp
from jax import lax
from jax.sharding import PartitionSpec as P


def slope(pre):
    sig = jax.nn.sigmoid(pre)
    return sig * (1.0 + pre * (1.0 - sig))


def contract(left, right, left_dim, right_dim):
    return lax.dot_general(
        left, right, (((left_dim,), (right_dim,)), ((), ())), preferred_element_type=jnp.float32
    )


def local(tokens, cotangent, norm_gain, expert_ids, combine_weight, up_weight, down_weight):
    n_expert = lax.axis_size("expert")
    groups = n_expert // 2
    count, piece = tokens.shape
    width = piece * lax.axis_size("dp")
    capacity = count * 5 // (4 * groups)
    token_f = tokens.astype(jnp.float32)
    squares = lax.psum(jnp.sum(token_f * token_f, axis=1, keepdims=True), "dp")
    scale = lax.rsqrt(squares / width + 1e-06)
    normed = (token_f * scale * norm_gain[None, :]).astype(jnp.bfloat16)
    scaled = (combine_weight[:, None] * cotangent.astype(jnp.float32)).astype(jnp.bfloat16)
    target = expert_ids[:, 0]
    hits = (target[:, None] == jnp.arange(groups, dtype=jnp.int32)[None, :]).astype(jnp.int32)
    slot = jnp.sum((jnp.cumsum(hits, axis=0) - 1) * hits, axis=1)
    flat_slot = target * capacity + slot
    places = (flat_slot[:, None] == jnp.arange(groups * capacity, dtype=jnp.int32)[None, :]).astype(
        jnp.bfloat16
    )
    packed_x = contract(places, normed, 0, 0).astype(jnp.bfloat16)
    packed_d = contract(places, scaled, 0, 0).astype(jnp.bfloat16)

    def outward(packed):
        return jnp.repeat(packed.reshape(groups, capacity, piece), 2, axis=0)

    sent_x, sent_d = (
        lax.all_to_all(outward(packed_x), "expert", split_axis=0, concat_axis=0, tiled=True),
        lax.all_to_all(outward(packed_d), "expert", split_axis=0, concat_axis=0, tiled=True),
    )
    rows_x = sent_x.reshape(-1, piece)
    rows_d = sent_d.reshape(-1, piece)
    full_up, full_down = (
        lax.all_gather(up_weight, "tensor", axis=1, tiled=True),
        lax.all_gather(down_weight, "tensor", axis=0, tiled=True),
    )
    up_part = jnp.dot(rows_x, full_up, preferred_element_type=jnp.float32)
    back_part = contract(rows_d, full_down, 1, 1)
    pre, back = (
        lax.psum(up_part.astype(jnp.bfloat16), "dp").astype(jnp.float32),
        lax.psum(back_part.astype(jnp.bfloat16), "dp").astype(jnp.float32),
    )
    act = jax.nn.silu(pre).astype(jnp.bfloat16)
    dpre = (back * slope(pre)).astype(jnp.bfloat16)
    down_terms = contract(act, rows_d, 0, 0)
    up_terms = contract(rows_x, dpre, 0, 0)
    down_sum, up_sum = (
        lax.psum_scatter(
            down_terms.astype(jnp.bfloat16), "tensor", scatter_dimension=0, tiled=True
        ).astype(jnp.float32),
        lax.psum_scatter(
            up_terms.astype(jnp.bfloat16), "tensor", scatter_dimension=1, tiled=True
        ).astype(jnp.float32),
    )
    down_grad = down_sum.astype(jnp.bfloat16)
    up_grad = up_sum.astype(jnp.bfloat16)
    row_grad = contract(dpre, full_up, 1, 1).astype(jnp.bfloat16)
    returned = lax.all_to_all(
        row_grad.reshape(n_expert, capacity, piece),
        "expert",
        split_axis=0,
        concat_axis=0,
        tiled=True,
    )
    returned = returned.reshape(groups, 2, capacity, piece).astype(jnp.float32)
    merged = (returned[:, 0] + returned[:, 1]).reshape(groups * capacity, piece)
    normed_grad = jnp.take(merged, flat_slot, axis=0)
    gain_terms = jnp.sum(normed_grad * token_f * scale, axis=0)
    gain_grad = lax.psum(gain_terms, ("expert", "tensor"))
    inner_part = jnp.sum(token_f * norm_gain[None, :] * normed_grad, axis=1, keepdims=True)
    inner = lax.psum(inner_part, "dp")
    cubed = scale * scale * scale
    token_grad = (
        cotangent.astype(jnp.float32)
        + scale * norm_gain[None, :] * normed_grad
        - token_f * cubed * inner / width
    )
    return (token_grad.astype(jnp.bfloat16), up_grad, down_grad, gain_grad, inner[:, 0])


def swap(value, axis):
    return lax.ppermute(value, axis, ((0, 1), (1, 0)))


def tie(*values):
    return lax.optimization_barrier(values)


def rounded(value):
    return value.astype(jnp.bfloat16)


def local_line(
    tokens, cotangent, norm_gain, expert_ids, combine_weight, up_weight, down_weight
):
    count, piece = tokens.shape
    width = piece * 2
    capacity = count * 5 // 8
    inward, middle, outward = ((0, 1), (3, 2)), ((1, 2), (2, 1)), ((1, 0), (2, 3))
    place = lax.axis_index("expert")
    mine = place // 2
    is_inner = (place == 1) | (place == 2)
    part = lax.axis_index("parts")
    side = lax.axis_index("tensor")

    def along(value, pairs):
        return lax.ppermute(value, "expert", pairs)

    def half(weight):
        size = weight.shape[0] // 2
        return lax.dynamic_slice_in_dim(weight, part * size, size, 0)

    tokens_in = along(tokens, inward)
    up_own = lax.all_gather(up_weight, "tensor", axis=1, tiled=True)
    down_own = lax.all_gather(down_weight, "tensor", axis=0, tiled=True)
    token_f = tokens.astype(jnp.float32)
    squares = lax.psum(jnp.sum(token_f * token_f, axis=1), "dp")
    scale = lax.rsqrt(squares / width + 1e-06)
    small = jnp.stack([scale, combine_weight, expert_ids[:, 0].astype(jnp.float32)])
    small_in = along(small, inward)

    def places(facts, expert):
        hit = facts[2].astype(jnp.int32) == expert
        slot = jnp.where(hit, jnp.cumsum(hit.astype(jnp.int32)) - 1, -1)
        return rounded(slot[:, None] == jnp.arange(capacity, dtype=jnp.int32)[None, :])

    def normed_of(block, facts):
        return rounded(block.astype(jnp.float32) * facts[0][:, None] * norm_gain[None, :])

    def scaled_of(block, facts):
        return rounded(facts[1][:, None] * block.astype(jnp.float32))

    def picked(where, rows):
        return rounded(contract(where, rows, 0, 0))

    keep_a, send_a = places(small, mine), places(small, 1 - mine)
    normed_a, scaled_a = normed_of(tokens, small), scaled_of(cotangent, small)
    far_xa = along(picked(send_a, normed_a), middle)
    near_xa, near_da = picked(keep_a, normed_a), picked(keep_a, scaled_a)
    send_da = picked(send_a, scaled_a)
    half_up, tokens_in, far_xa, send_da, near_xa, near_da, small_in = tie(
        half(up_weight), tokens_in, far_xa, send_da, near_xa, near_da, small_in
    )

    up_in = along(half_up, inward)
    far_da = along(send_da, middle)
    keep_b, send_b = places(small_in, mine), places(small_in, 1 - mine)
    normed_b = normed_of(tokens_in, small_in)
    send_xb, near_xb = picked(send_b, normed_b), picked(keep_b, normed_b)
    half_down, up_in, far_da, send_xb, near_xb = tie(
        half(down_weight), up_in, far_da, send_xb, near_xb
    )

    down_in = along(half_down, inward)
    far_xb = along(send_xb, middle)
    up_other = swap(up_in, "parts")
    cot_sent, down_in, far_xb, up_other = tie(cotangent, down_in, far_xb, up_other)

    cotangent_in = along(cot_sent, inward)
    down_other = swap(down_in, "parts")

    def joined(here, there):
        first, second = jnp.where(part == 0, here, there), jnp.where(part == 0, there, here)
        return jnp.concatenate([first, second], axis=0)

    up_out = lax.all_gather(joined(up_in, up_other), "tensor", axis=1, tiled=True)
    cotangent_in, down_other, up_out = tie(cotangent_in, down_other, up_out)
    down_out = lax.all_gather(joined(down_in, down_other), "tensor", axis=0, tiled=True)
    rows_x = jnp.concatenate([far_xa, near_xa, near_xb, far_xb])

    def over_dp(value):
        return value.astype(jnp.float32) + swap(value, "dp").astype(jnp.float32)

    pre_own = rounded(contract(rows_x, up_own, 1, 0))
    pre_out = rounded(contract(rows_x, up_out, 1, 0))
    pre = jnp.concatenate([over_dp(pre_own), over_dp(pre_out)], axis=1)

    scaled_b = scaled_of(cotangent_in, small_in)
    far_db = along(picked(send_b, scaled_b), middle)
    early = jnp.concatenate([far_da, near_da, picked(keep_b, scaled_b)])

    def back_of(rows):
        parts_of = [contract(rows, down_own, 1, 1), contract(rows, down_out, 1, 1)]
        return over_dp(rounded(jnp.concatenate(parts_of, axis=1)))

    back = jnp.concatenate([back_of(early), back_of(far_db)])
    rows_d = jnp.concatenate([early, far_db])
    act = rounded(jax.nn.silu(pre))
    dpre = rounded(back * slope(pre))
    unit = act.shape[1] // 2

    def row_grad(rows):
        own = contract(rows[:, :unit], up_own, 1, 1)
        return rounded(own + contract(rows[:, unit:], up_out, 1, 1))

    back_b = along(row_grad(dpre[3 * capacity :]), middle)
    back_a = along(row_grad(dpre[:capacity]), middle)
    near_grad = row_grad(dpre[capacity : 3 * capacity])

    def shared(terms, axis):
        size = terms.shape[axis] // 2
        own = lax.dynamic_slice_in_dim(terms, side * size, size, axis)
        other = lax.dynamic_slice_in_dim(terms, (1 - side) * size, size, axis)
        return rounded(own + swap(rounded(other), "tensor").astype(jnp.float32))

    down_far = along(shared(contract(act[:, unit:], rows_d, 0, 0), 0), outward)
    up_far = along(shared(contract(rows_x, dpre[:, unit:], 0, 0), 1), outward)
    down_near = shared(contract(act[:, :unit], rows_d, 0, 0), 0)
    up_near = shared(contract(rows_x, dpre[:, :unit], 0, 0), 1)

    def restored(keep, near, send, far):
        return rounded(contract(keep, near, 1, 0) + contract(send, far, 1, 0))

    back_a, down_far = tie(back_a, down_far)
    grad_b = restored(keep_b, near_grad[capacity:], send_b, back_b)
    grad_in = along(grad_b, outward)
    grad_a = restored(keep_a, near_grad[:capacity], send_a, back_a)

    def gain_of(grad, block, facts):
        block = block.astype(jnp.float32) * facts[0][:, None]
        return jnp.sum(grad.astype(jnp.float32) * block, axis=0)

    def inner_of(grad, block):
        gained = block.astype(jnp.float32) * norm_gain[None, :]
        return jnp.sum(gained * grad.astype(jnp.float32), axis=1)

    gain_terms = gain_of(grad_a, tokens, small) + gain_of(grad_b, tokens_in, small_in)
    gain_terms = gain_terms + swap(gain_terms, "tensor")
    gain_terms = gain_terms + along(gain_terms, middle)
    gain_grad = jnp.where(is_inner, gain_terms, along(gain_terms, outward))
    inner_ab = jnp.stack([inner_of(grad_a, tokens), inner_of(grad_b, tokens_in)])
    inner_ab = over_dp(inner_ab)
    inner = jnp.where(is_inner, inner_ab[0], along(inner_ab[1], outward))
    normed_grad = jnp.where(is_inner, grad_a, grad_in).astype(jnp.float32)
    scale = scale[:, None]
    cubed = scale * scale * scale
    token_grad = (
        cotangent.astype(jnp.float32)
        + scale * norm_gain[None, :] * normed_grad
        - token_f * cubed * inner[:, None] / width
    )
    up_grad = jnp.where(is_inner, up_near, up_far)
    down_grad = jnp.where(is_inner, down_near, down_far)
    return (rounded(token_grad), up_grad, down_grad, gain_grad, inner)


def solution(mesh):
    sizes = tuple(mesh.shape[name] for name in ("parts", "expert", "dp", "tensor"))
    body = local_line if sizes == (2, 4, 2, 2) else local
    in_specs = (
        P(("parts", "expert", "tensor"), "dp"),
        P(("parts", "expert", "tensor"), "dp"),
        P("dp"),
        P(("parts", "expert", "tensor"), None),
        P(("parts", "expert", "tensor")),
        P("dp", ("expert", "tensor")),
        P(("expert", "tensor"), "dp"),
    )
    out_specs = (
        P(("parts", "expert", "tensor"), "dp"),
        P(("parts", "dp"), ("expert", "tensor")),
        P(("parts", "expert", "tensor"), "dp"),
        P(("parts", "dp")),
        P(("parts", "expert", "tensor")),
    )
    return jax.shard_map(body, mesh=mesh, in_specs=in_specs, out_specs=out_specs, check_vma=False)
```

profile of v0, /device:TPU:0, one launch (start us, length us, event | category | flops | bytes accessed | tf_op | source)
XLA Modules:
  0.0 418.2 jit_solution(5469492029887555901)
XLA Ops:
  7.2 6.3 %collective-permute-start = (bf16[256,3584]{1,0:T(8,128)(2,1)}, bf16[256,3584]{1,0:T(8,128)(2,1)}, u32[]{:S(2)}, u32[]{:S(2)}) collective-permute-start(bf16[256,3584]{1,0:T(8,128)(2,1)} %param.7), channel_id=1, source_target_pairs={{0,4},{12,8},{1,5},{13,9},{2,6},{14,10},{3,7},{15,11},{16,20},{28,... | collective-permute-start | bytes 5505032 | tf_op jit(solution)/shard_map/ppermute | solution.py:122
  15.5 4.9 %psum.7 = f32[256]{0:T(256)S(1)} all-reduce(f32[256]{0:T(256)S(1)} %fusion.16), channel_id=1, replica_groups=mesh['parts'=2,'expert'=4,'dp'=2,'tensor'=2] {'dp'}, use_global_device_ids=true, to_apply=%region_1.2 | all-reduce | flops 256 | bytes 2048 | tf_op jit(solution)/shard_map/psum | solution.py:132
  32.3 3.4 convolution_convert_fusion.5
  38.9 13.0 %collective-permute-done.2 = f32[3,256]{1,0:T(4,128)S(1)} collective-permute-done((f32[3,256]{1,0:T(4,128)S(1)}, f32[3,256]{1,0:T(4,128)S(1)}, u32[]{:S(2)}, u32[]{:S(2)}) %collective-permute-start.2) | collective-permute-done | bytes 3104 | tf_op jit(solution)/shard_map/ppermute | solution.py:122
  51.9 5.3 %collective-permute-start.3 = (bf16[1792,256]{1,0:T(8,128)(2,1)}, bf16[1792,256]{1,0:T(8,128)(2,1)}, u32[]{:S(2)}, u32[]{:S(2)}) collective-permute-start(bf16[1792,256]{1,0:T(8,128)(2,1)} %constant_dynamic-slice_fusion), channel_id=1, source_target_pairs={{0,4},{12,8},{1,5},{13,9},{2,6},{14,10},{3,7},{15,11},{16,20},{28,... | collective-permute-start | bytes 2752520 | tf_op jit(solution)/shard_map/ppermute | solution.py:122
  66.7 8.7 %collective-permute-done.3 = bf16[1792,256]{1,0:T(8,128)(2,1)} collective-permute-done((bf16[1792,256]{1,0:T(8,128)(2,1)}, bf16[1792,256]{1,0:T(8,128)(2,1)}, u32[]{:S(2)}, u32[]{:S(2)}) %collective-permute-start.3) | collective-permute-done | bytes 917536 | tf_op jit(solution)/shard_map/ppermute | solution.py:122
  76.1 14.1 %collective-permute-start.5 = (bf16[128,3584]{1,0:T(8,128)(2,1)}, bf16[128,3584]{1,0:T(8,128)(2,1)}, u32[]{:S(2)}, u32[]{:S(2)}) collective-permute-start(bf16[128,3584]{1,0:T(8,128)(2,1)} %constant_dynamic-slice_fusion.1), channel_id=1, source_target_pairs={{0,4},{12,8},{1,5},{13,9},{2,6},{14,10},{3,7},{15,11},{16,20},{28,... | collective-permute-start | bytes 2752520 | tf_op jit(solution)/shard_map/ppermute | solution.py:122
  91.7 15.4 %collective-permute-done.5 = bf16[128,3584]{1,0:T(8,128)(2,1)} collective-permute-done((bf16[128,3584]{1,0:T(8,128)(2,1)}, bf16[128,3584]{1,0:T(8,128)(2,1)}, u32[]{:S(2)}, u32[]{:S(2)}) %collective-permute-start.5) | collective-permute-done | bytes 917536 | tf_op jit(solution)/shard_map/ppermute | solution.py:122
  115.2 4.1 collective-permute-start.8
  124.5 14.3 %collective-permute-done.9 = bf16[128,3584]{1,0:T(8,128)(2,1)} collective-permute-done((bf16[128,3584]{1,0:T(8,128)(2,1)}, bf16[128,3584]{1,0:T(8,128)(2,1)}, u32[]{:S(2)}, u32[]{:S(2)}) %collective-permute-start.9) | collective-permute-done | bytes 917536 | tf_op jit(solution)/shard_map/ppermute | solution.py:97
  138.9 15.9 %collective-permute-done.8 = bf16[256,3584]{1,0:T(8,128)(2,1)} collective-permute-done((bf16[256,3584]{1,0:T(8,128)(2,1)S(1)}, bf16[256,3584]{1,0:T(8,128)(2,1)}, u32[]{:S(2)}, u32[]{:S(2)}) %collective-permute-start.8) | collective-permute-done | bytes 1835040 | tf_op jit(solution)/shard_map/ppermute | solution.py:122
  160.9 6.9 %convolution_convert_fusion.9 = bf16[640,512]{1,0:T(8,128)(2,1)} fusion(bf16[640,3584]{1,0:T(8,128)(2,1)} %constant_dynamic-update-slice_fusion, bf16[3584,512]{1,0:T(8,128)(2,1)} %all-gather.11.cloned.1.call-done), kind=kOutput, calls=%fused_computation.68 | convolution fusion | flops 2349137920 | bytes 8912896 | tf_op jit(solution)/shard_map/dot_general | solution.py:13
  169.3 3.6 convolution_convert_fusion
  180.7 5.2 %fusion.24 = bf16[480,512]{1,0:T(8,128)(2,1)S(1)} fusion(bf16[512,3584]{1,0:T(8,128)(2,1)} %all-gather.7.cloned.1.call-done, bf16[160,3584]{1,0:T(8,128)(2,1)} %convolution_convert_fusion.1, bf16[160,3584]{1,0:T(8,128)(2,1)} %convolution_convert_fusion.4, bf16[160,3584]{1,0:T(8,128)(2,1)} %collective-permute-done.4), kind=kOutput, calls=%fused_computation.71 | convolution fusion | flops 1772175360 | bytes 7602176 | tf_op jit(solution)/shard_map/dot_general | solution.py:13
  187.9 5.2 %fusion.25 = bf16[480,512]{1,0:T(8,128)(2,1)S(1)} fusion(bf16[512,3584]{1,0:T(8,128)(2,1)} %all-gather.9.cloned.1.call-done, bf16[160,3584]{1,0:T(8,128)(2,1)} %convolution_convert_fusion.1, bf16[160,3584]{1,0:T(8,128)(2,1)} %convolution_convert_fusion.4, bf16[160,3584]{1,0:T(8,128)(2,1)} %collective-permute-done.4), kind=kOutput, calls=%fused_computation.72 | convolution fusion | flops 1772175360 | bytes 7602176 | tf_op jit(solution)/shard_map/dot_general | solution.py:13
  200.4 23.1 %collective-permute-done.12 = bf16[160,1024]{1,0:T(8,128)(2,1)S(1)} collective-permute-done((bf16[160,1024]{1,0:T(8,128)(2,1)S(1)}, bf16[160,1024]{1,0:T(8,128)(2,1)S(1)}, u32[]{:S(2)}, u32[]{:S(2)}) %collective-permute-start.12) | collective-permute-done | bytes 327712 | tf_op jit(solution)/shard_map/ppermute | solution.py:97
  246.8 4.3 %fusion.31 = f32[512,3584]{1,0:T(8,128)S(1)} fusion(bf16[160,3584]{1,0:T(8,128)(2,1)S(1)} %collective-permute-done.11, bf16[160,3584]{1,0:T(8,128)(2,1)S(1)} %copy-done.13, bf16[160,3584]{1,0:T(8,128)(2,1)S(1)} %copy-done.12, bf16[160,3584]{1,0:T(8,128)(2,1)} %collective-permute-done.4, bf16[640,1024]{1,0:T(8,128)(2,1)S(1)} %get-tuple-element.53), kind=kOutput, calls=%fused_computation.85 | convolution fusion | flops 2367160320 | bytes 12582912 | tf_op jit(solution)/shard_map/dot_general | solution.py:13
  255.3 5.0 %fusion.37 = f32[3584,512]{1,0:T(8,128)S(1)} fusion(bf16[640,3584]{1,0:T(8,128)(2,1)} %constant_dynamic-update-slice_fusion, bf16[640,1024]{1,0:T(8,128)(2,1)S(1)} %get-tuple-element.54), kind=kOutput, calls=%fused_computation.89 | convolution fusion | flops 2348810240 | bytes 12582912 | tf_op jit(solution)/shard_map/dot_general | solution.py:13
  262.3 5.5 %fusion.30 = f32[512,3584]{1,0:T(8,128)S(1)} fusion(bf16[160,3584]{1,0:T(8,128)(2,1)S(1)} %collective-permute-done.11, bf16[160,3584]{1,0:T(8,128)(2,1)} %convolution_convert_fusion.1, bf16[160,3584]{1,0:T(8,128)(2,1)} %convolution_convert_fusion.4, bf16[160,3584]{1,0:T(8,128)(2,1)} %collective-permute-done.4, bf16[640,1024]{1,0:T(8,128)(2,1)} %copy-done.11), kind=kOutput, calls=%fused_computation.84 | convolution fusion | flops 2367160320 | bytes 12582912 | tf_op jit(solution)/shard_map/dot_general | solution.py:13
  280.4 46.7 %collective-permute-done.17 = bf16[256,3584]{1,0:T(8,128)(2,1)S(1)} collective-permute-done((bf16[256,3584]{1,0:T(8,128)(2,1)S(1)}, bf16[256,3584]{1,0:T(8,128)(2,1)S(1)}, u32[]{:S(2)}, u32[]{:S(2)}) %collective-permute-start.17) | collective-permute-done | bytes 1835040 | tf_op jit(solution)/shard_map/ppermute | solution.py:122
  327.1 4.7 %fusion.13 = (f32[3584]{0:T(1024)S(1)}, f32[256]{0:T(256)S(1)}, f32[256]{0:T(256)S(1)}, f32[3584]{0:T(1024)S(1)}, bf16[256,3584]{1,0:T(8,128)(2,1)S(1)}) fusion(bf16[256,3584]{1,0:T(8,128)(2,1)S(1)} %copy-done.4, f32[256]{0:T(256)S(1)} %get-tuple-element.70, f32[3584]{0:T(1024)S(1)} %copy-done.20, f32[256]{0:T(256)S(1)} %bitcast.69, ...), kind=kOutput, calls=%fused_computation.39 | convolution fusion | flops 310149632 | bytes 12205056 | tf_op jit(solution)/shard_map/dot_general | solution.py:13
  332.2 34.2 %collective-permute-done.24 = bf16[3584,256]{1,0:T(8,128)(2,1)S(1)} collective-permute-done((bf16[3584,256]{1,0:T(8,128)(2,1)S(1)}, bf16[3584,256]{1,0:T(8,128)(2,1)S(1)}, u32[]{:S(2)}, u32[]{:S(2)}) %collective-permute-start.24) | collective-permute-done | bytes 1835040 | tf_op jit(solution)/shard_map/ppermute | solution.py:122
  366.4 3.6 fusion.20
  374.0 30.9 %collective-permute-done.21 = f32[256]{0:T(256)S(1)} collective-permute-done((f32[256]{0:T(256)S(1)}, f32[256]{0:T(256)S(1)}, u32[]{:S(2)}, u32[]{:S(2)}) %collective-permute-start.21) | collective-permute-done | bytes 1056 | tf_op jit(solution)/shard_map/ppermute | solution.py:122
  (191 shorter events, 118.9 us)
Async XLA Ops:
  7.2 147.6 %all-gather.5.cloned.1.call-start = ((), (), s32[]{:S(2)}) async-start(), calls=%async_computation | async-start | bytes 5505024 | tf_op jit(solution)/shard_map/all_gather | solution.py:181
  7.2 44.7 %collective-permute-start = (bf16[256,3584]{1,0:T(8,128)(2,1)}, bf16[256,3584]{1,0:T(8,128)(2,1)}, u32[]{:S(2)}, u32[]{:S(2)}) collective-permute-start(bf16[256,3584]{1,0:T(8,128)(2,1)} %param.7), channel_id=1, source_target_pairs={{0,4},{12,8},{1,5},{13,9},{2,6},{14,10},{3,7},{15,11},{16,20},{28,... | collective-permute-start | bytes 5505032 | tf_op jit(solution)/shard_map/ppermute | solution.py:122
  26.3 25.6 %collective-permute-start.1 = (bf16[160,3584]{1,0:T(8,128)(2,1)}, bf16[160,3584]{1,0:T(8,128)(2,1)}, u32[]{:S(2)}, u32[]{:S(2)}) collective-permute-start(bf16[160,3584]{1,0:T(8,128)(2,1)} %convolution_convert_fusion.7), channel_id=1, source_target_pairs={{4,8},{8,4},{5,9},{9,5},{6,10},{10,6},{7,11},{11,7},{20,24},{24,20... | collective-permute-start | bytes 3440648 | tf_op jit(solution)/shard_map/ppermute | solution.py:122
  28.0 23.9 %collective-permute-start.2 = (f32[3,256]{1,0:T(4,128)S(1)}, f32[3,256]{1,0:T(4,128)S(1)}, u32[]{:S(2)}, u32[]{:S(2)}) collective-permute-start(f32[3,256]{1,0:T(4,128)S(1)} %pad_maximum_fusion.15), channel_id=1, source_target_pairs={{0,4},{12,8},{1,5},{13,9},{2,6},{14,10},{3,7},{15,11},{16,20},{28,... | collective-permute-start | bytes 9224 | tf_op jit(solution)/shard_map/ppermute | solution.py:122
  75.4 34.9 %collective-permute-start.6 = (bf16[160,3584]{1,0:T(8,128)(2,1)}, bf16[160,3584]{1,0:T(8,128)(2,1)S(1)}, u32[]{:S(2)}, u32[]{:S(2)}) collective-permute-start(bf16[160,3584]{1,0:T(8,128)(2,1)} %convolution_convert_fusion.3), channel_id=1, source_target_pairs={{4,8},{8,4},{5,9},{9,5},{6,10},{10,6},{7,11},{11,7},{20,24},{24,20... | collective-permute-start | bytes 3440648 | tf_op jit(solution)/shard_map/ppermute | solution.py:122
  76.1 31.0 %collective-permute-start.5 = (bf16[128,3584]{1,0:T(8,128)(2,1)}, bf16[128,3584]{1,0:T(8,128)(2,1)}, u32[]{:S(2)}, u32[]{:S(2)}) collective-permute-start(bf16[128,3584]{1,0:T(8,128)(2,1)} %constant_dynamic-slice_fusion.1), channel_id=1, source_target_pairs={{0,4},{12,8},{1,5},{13,9},{2,6},{14,10},{3,7},{15,11},{16,20},{28,... | collective-permute-start | bytes 2752520 | tf_op jit(solution)/shard_map/ppermute | solution.py:122
  113.7 47.2 %all-gather.11.cloned.1.call-start = ((), (), s32[]{:S(2)}) async-start(), calls=%async_computation.3 | async-start | bytes 5505024 | tf_op jit(solution)/shard_map/all_gather | solution.py:129
  114.4 66.2 %all-gather.7.cloned.1.call-start = ((), (), s32[]{:S(2)}) async-start(), calls=%async_computation.1 | async-start | bytes 5505024 | tf_op jit(solution)/shard_map/all_gather | solution.py:130
  115.2 72.7 %all-gather.9.cloned.1.call-start = ((), (), s32[]{:S(2)}) async-start(), calls=%async_computation.2 | async-start | bytes 5505024 | tf_op jit(solution)/shard_map/all_gather | solution.py:183
  115.2 39.5 %collective-permute-start.8 = (bf16[256,3584]{1,0:T(8,128)(2,1)S(1)}, bf16[256,3584]{1,0:T(8,128)(2,1)}, u32[]{:S(2)}, u32[]{:S(2)}) collective-permute-start(bf16[256,3584]{1,0:T(8,128)(2,1)S(1)} %copy-done.3), channel_id=1, source_target_pairs={{0,4},{12,8},{1,5},{13,9},{2,6},{14,10},{3,7},{15,11},{16,20},{28,... | collective-permute-start | bytes 5505032 | tf_op jit(solution)/shard_map/ppermute | solution.py:122
  167.8 29.0 %collective-permute-start.13 = (bf16[640,512]{1,0:T(8,128)(2,1)}, bf16[640,512]{1,0:T(8,128)(2,1)}, u32[]{:S(2)}, u32[]{:S(2)}) collective-permute-start(bf16[640,512]{1,0:T(8,128)(2,1)} %convolution_convert_fusion.9), channel_id=1, source_target_pairs={{0,2},{2,0},{1,3},{3,1},{4,6},{6,4},{5,7},{7,5},{8,10},{10,8},{9,1... | collective-permute-start | bytes 1966088 | tf_op jit(solution)/shard_map/ppermute | solution.py:97
  193.2 30.4 %collective-permute-start.10 = (bf16[480,1024]{1,0:T(8,128)(2,1)S(1)}, bf16[480,1024]{1,0:T(8,128)(2,1)S(1)}, u32[]{:S(2)}, u32[]{:S(2)}) collective-permute-start(bf16[480,1024]{1,0:T(8,128)(2,1)S(1)} %pad_maximum_fusion.11), channel_id=1, source_target_pairs={{0,2},{2,0},{1,3},{3,1},{4,6},{6,4},{5,7},{7,5},{8,10},{10,8},{9,1... | collective-permute-start | bytes 2949128 | tf_op jit(solution)/shard_map/ppermute | solution.py:97
  196.3 27.2 %collective-permute-start.12 = (bf16[160,1024]{1,0:T(8,128)(2,1)S(1)}, bf16[160,1024]{1,0:T(8,128)(2,1)S(1)}, u32[]{:S(2)}, u32[]{:S(2)}) collective-permute-start(bf16[160,1024]{1,0:T(8,128)(2,1)S(1)} %pad_maximum_fusion.14), channel_id=1, source_target_pairs={{0,2},{2,0},{1,3},{3,1},{4,6},{6,4},{5,7},{7,5},{8,10},{10,8},{9,1... | collective-permute-start | bytes 983048 | tf_op jit(solution)/shard_map/ppermute | solution.py:97
  239.8 37.1 %collective-permute-start.18 = (bf16[160,3584]{1,0:T(8,128)(2,1)}, bf16[160,3584]{1,0:T(8,128)(2,1)}, u32[]{:S(2)}, u32[]{:S(2)}) collective-permute-start(bf16[160,3584]{1,0:T(8,128)(2,1)} %fusion.4), channel_id=1, source_target_pairs={{4,8},{8,4},{5,9},{9,5},{6,10},{10,6},{7,11},{11,7},{20,24},{24,20... | collective-permute-start | bytes 3440648 | tf_op jit(solution)/shard_map/ppermute | solution.py:122
  245.2 33.9 %collective-permute-start.15 = (bf16[160,3584]{1,0:T(8,128)(2,1)}, bf16[160,3584]{1,0:T(8,128)(2,1)}, u32[]{:S(2)}, u32[]{:S(2)}) collective-permute-start(bf16[160,3584]{1,0:T(8,128)(2,1)} %fusion.3), channel_id=1, source_target_pairs={{4,8},{8,4},{5,9},{9,5},{6,10},{10,6},{7,11},{11,7},{20,24},{24,20... | collective-permute-start | bytes 3440648 | tf_op jit(solution)/shard_map/ppermute | solution.py:122
  261.8 70.4 %collective-permute-start.22 = (bf16[3584,256]{1,0:T(8,128)(2,1)}, bf16[3584,256]{1,0:T(8,128)(2,1)}, u32[]{:S(2)}, u32[]{:S(2)}) collective-permute-start(bf16[3584,256]{1,0:T(8,128)(2,1)} %dynamic-slice_convert_fusion.2), channel_id=1, source_target_pairs={{0,1},{1,0},{2,3},{3,2},{4,5},{5,4},{6,7},{7,6},{8,9},{9,8},{10,11... | collective-permute-start | bytes 5505032 | tf_op jit(solution)/shard_map/ppermute | solution.py:97
  270.9 56.2 %collective-permute-start.17 = (bf16[256,3584]{1,0:T(8,128)(2,1)S(1)}, bf16[256,3584]{1,0:T(8,128)(2,1)S(1)}, u32[]{:S(2)}, u32[]{:S(2)}) collective-permute-start(bf16[256,3584]{1,0:T(8,128)(2,1)S(1)} %add_convert_fusion.3), channel_id=1, source_target_pairs={{4,0},{8,12},{5,1},{9,13},{6,2},{10,14},{7,3},{11,15},{20,16},{24,... | collective-permute-start | bytes 5505032 | tf_op jit(solution)/shard_map/ppermute | solution.py:122
  274.7 91.7 %collective-permute-start.24 = (bf16[3584,256]{1,0:T(8,128)(2,1)S(1)}, bf16[3584,256]{1,0:T(8,128)(2,1)S(1)}, u32[]{:S(2)}, u32[]{:S(2)}) collective-permute-start(bf16[3584,256]{1,0:T(8,128)(2,1)S(1)} %add_convert_fusion.1), channel_id=1, source_target_pairs={{4,0},{8,12},{5,1},{9,13},{6,2},{10,14},{7,3},{11,15},{20,16},{24,... | collective-permute-start | bytes 5505032 | tf_op jit(solution)/shard_map/ppermute | solution.py:122
  276.9 94.5 %collective-permute-start.25 = (bf16[256,3584]{1,0:T(8,128)(2,1)S(1)}, bf16[256,3584]{1,0:T(8,128)(2,1)S(1)}, u32[]{:S(2)}, u32[]{:S(2)}) collective-permute-start(bf16[256,3584]{1,0:T(8,128)(2,1)S(1)} %dynamic-slice_convert_fusion), channel_id=1, source_target_pairs={{0,1},{1,0},{2,3},{3,2},{4,5},{5,4},{6,7},{7,6},{8,9},{9,8},{10,11... | collective-permute-start | bytes 5505032 | tf_op jit(solution)/shard_map/ppermute | solution.py:97
  279.1 127.2 %collective-permute-start.19 = (bf16[256,3584]{1,0:T(8,128)(2,1)S(1)}, bf16[256,3584]{1,0:T(8,128)(2,1)S(1)}, u32[]{:S(2)}, u32[]{:S(2)}) collective-permute-start(bf16[256,3584]{1,0:T(8,128)(2,1)S(1)} %fusion.2), channel_id=1, source_target_pairs={{4,0},{8,12},{5,1},{9,13},{6,2},{10,14},{7,3},{11,15},{20,16},{24,... | collective-permute-start | bytes 5505032 | tf_op jit(solution)/shard_map/ppermute | solution.py:122
  331.8 38.2 %collective-permute-start.20 = (f32[2,256]{1,0:T(2,128)S(1)}, f32[2,256]{1,0:T(2,128)S(1)}, u32[]{:S(2)}, u32[]{:S(2)}) collective-permute-start(f32[2,256]{1,0:T(2,128)S(1)} %pad_maximum_fusion.16), channel_id=1, source_target_pairs={{0,2},{2,0},{1,3},{3,1},{4,6},{6,4},{5,7},{7,5},{8,10},{10,8},{9,1... | collective-permute-start | bytes 6152 | tf_op jit(solution)/shard_map/ppermute | solution.py:97
  332.2 41.2 %collective-permute-start.26 = (f32[3584]{0:T(1024)S(1)}, f32[3584]{0:T(1024)S(1)}, u32[]{:S(2)}, u32[]{:S(2)}) collective-permute-start(f32[3584]{0:T(1024)S(1)} %add.142), channel_id=1, source_target_pairs={{0,1},{1,0},{2,3},{3,2},{4,5},{5,4},{6,7},{7,6},{8,9},{9,8},{10,11... | collective-permute-start | bytes 43016 | tf_op jit(solution)/shard_map/ppermute | solution.py:97
  370.1 34.9 %collective-permute-start.21 = (f32[256]{0:T(256)S(1)}, f32[256]{0:T(256)S(1)}, u32[]{:S(2)}, u32[]{:S(2)}) collective-permute-start(f32[256]{0:T(256)S(1)} %bitcast.70), channel_id=1, source_target_pairs={{4,0},{8,12},{5,1},{9,13},{6,2},{10,14},{7,3},{11,15},{20,16},{24,... | collective-permute-start | bytes 3080 | tf_op jit(solution)/shard_map/ppermute | solution.py:122
  373.3 31.6 %collective-permute-start.27 = (f32[3584]{0:T(1024)S(1)}, f32[3584]{0:T(1024)S(1)}, u32[]{:S(2)}, u32[]{:S(2)}) collective-permute-start(f32[3584]{0:T(1024)S(1)} %add.143), channel_id=1, source_target_pairs={{4,8},{8,4},{5,9},{9,5},{6,10},{10,6},{7,11},{11,7},{20,24},{24,20... | collective-permute-start | bytes 43016 | tf_op jit(solution)/shard_map/ppermute | solution.py:122
  (36 other events, 413.0 us)
Sparse Core Ops, SparseCore 0:
  113.8 11.8 all-gather.4
  127.3 13.4 all-gather.10
  142.4 14.0 all-gather.6
  158.5 14.0 all-gather.8
where the time goes:
time: 426 us; the launch traced here: 418 us
  waiting for transfers between devices  209 us (49%)
  matrix products  82.8 us (19%)
  starting transfers between devices  55.6 us (13%)
  other arithmetic  30.5 us (7%)
  local copies, waits for them, and re-layouts  20.7 us (5%)
  between operations  14.8 us (3%)
  blocking collectives  4.94 us (1%)
    ppermute x17, waiting for transfers between devices, along(): return lax.ppermute(value, 'expert', pairs)  166 us
    dot_general x28, matrix products, contract(): lax.dot_general(left, right, (((left_dim,), (right_dim,)), ((), ())), pre...  82.8 us
    ppermute x17, starting transfers between devices, along(): return lax.ppermute(value, 'expert', pairs)  47.4 us
    ppermute x12, waiting for transfers between devices, swap(): return lax.ppermute(value, axis, ((0, 1), (1, 0)))  41.3 us
    unnamed x57, local copies, waits for them, and re-layouts  10.4 us
    convert_element_type x4, other arithmetic, rounded(): return value.astype(jnp.bfloat16)  9.5 us
  transfers between devices with their start and end apart: 33, of which 12 were waited for; matrix products, arithmetic and copies ran while one was open for 26% of the time, Pallas kernels for 0%

commit v1 on v0

--- a/solution.py
+++ b/solution.py
@@ -226,7 +226,7 @@
     def restored(keep, near, send, far):
         return rounded(contract(keep, near, 1, 0) + contract(send, far, 1, 0))
 
-    back_a, down_far = tie(back_a, down_far)
+    back_b, back_a, down_far = tie(back_b, back_a, down_far)
     grad_b = restored(keep_b, near_grad[capacity:], send_b, back_b)
     grad_in = along(grad_b, outward)
     grad_a = restored(keep_a, near_grad[:capacity], send_a, back_a)

time: 426 us -> 426 us (level)
    unnamed x57 -> x67, local copies, waits for them, and re-layouts: 10.4 us -> 12.9 us
  transfers between devices with their start and end apart: 33 -> 33, of which waited for: 12 -> 12; matrix products, arithmetic and copies ran while one was open for 26% -> 28% of each run, Pallas kernels for 0% -> 0%
where the time goes in v1:
time: 426 us; the launch traced here: 418 us
  waiting for transfers between devices  205 us (48%)
  matrix products  83.1 us (20%)
  starting transfers between devices  53.6 us (13%)
  other arithmetic  32.3 us (8%)
  local copies, waits for them, and re-layouts  24 us (6%)
  between operations  14.9 us (3%)
  blocking collectives  4.92 us (1%)
    ppermute x17, waiting for transfers between devices, along(): return lax.ppermute(value, 'expert', pairs)  162 us
    dot_general x28, matrix products, contract(): lax.dot_general(left, right, (((left_dim,), (right_dim,)), ((), ())), pre...  83.1 us
    ppermute x17, starting transfers between devices, along(): return lax.ppermute(value, 'expert', pairs)  45.2 us
    ppermute x12, waiting for transfers between devices, swap(): return lax.ppermute(value, axis, ((0, 1), (1, 0)))  41.5 us
    unnamed x67, local copies, waits for them, and re-layouts  12.9 us
    convert_element_type x4, other arithmetic, rounded(): return value.astype(jnp.bfloat16)  11.1 us
  transfers between devices with their start and end apart: 33, of which 12 were waited for; matrix products, arithmetic and copies ran while one was open for 28% of the time, Pallas kernels for 0%

profile of v1, /device:TPU:0, one launch (start us, length us, event | category | flops | bytes accessed | tf_op | source)
XLA Modules:
  0.0 418.0 jit_solution(1813238481960670481)
XLA Ops:
  7.2 6.2 %collective-permute-start = (bf16[256,3584]{1,0:T(8,128)(2,1)}, bf16[256,3584]{1,0:T(8,128)(2,1)}, u32[]{:S(2)}, u32[]{:S(2)}) collective-permute-start(bf16[256,3584]{1,0:T(8,128)(2,1)} %param.7), channel_id=1, source_target_pairs={{0,4},{12,8},{1,5},{13,9},{2,6},{14,10},{3,7},{15,11},{16,20},{28,... | collective-permute-start | bytes 5505032 | tf_op jit(solution)/shard_map/ppermute | solution.py:122
  17.4 4.9 %psum.7 = f32[256]{0:T(256)S(1)} all-reduce(f32[256]{0:T(256)S(1)} %fusion.16), channel_id=1, replica_groups=mesh['parts'=2,'expert'=4,'dp'=2,'tensor'=2] {'dp'}, use_global_device_ids=true, to_apply=%region_1.2 | all-reduce | flops 256 | bytes 2048 | tf_op jit(solution)/shard_map/psum | solution.py:132
  32.2 3.4 convolution_convert_fusion.5
  38.9 12.9 %collective-permute-done.2 = f32[3,256]{1,0:T(4,128)S(1)} collective-permute-done((f32[3,256]{1,0:T(4,128)S(1)}, f32[3,256]{1,0:T(4,128)S(1)}, u32[]{:S(2)}, u32[]{:S(2)}) %collective-permute-start.2) | collective-permute-done | bytes 3104 | tf_op jit(solution)/shard_map/ppermute | solution.py:122
  53.4 8.1 %collective-permute-start.3 = (bf16[1792,256]{1,0:T(8,128)(2,1)}, bf16[1792,256]{1,0:T(8,128)(2,1)}, u32[]{:S(2)}, u32[]{:S(2)}) collective-permute-start(bf16[1792,256]{1,0:T(8,128)(2,1)} %constant_dynamic-slice_fusion), channel_id=1, source_target_pairs={{0,4},{12,8},{1,5},{13,9},{2,6},{14,10},{3,7},{15,11},{16,20},{28,... | collective-permute-start | bytes 2752520 | tf_op jit(solution)/shard_map/ppermute | solution.py:122
  68.4 10.9 %collective-permute-done.3 = bf16[1792,256]{1,0:T(8,128)(2,1)} collective-permute-done((bf16[1792,256]{1,0:T(8,128)(2,1)}, bf16[1792,256]{1,0:T(8,128)(2,1)}, u32[]{:S(2)}, u32[]{:S(2)}) %collective-permute-start.3) | collective-permute-done | bytes 917536 | tf_op jit(solution)/shard_map/ppermute | solution.py:122
  81.1 9.5 %collective-permute-start.5 = (bf16[128,3584]{1,0:T(8,128)(2,1)}, bf16[128,3584]{1,0:T(8,128)(2,1)}, u32[]{:S(2)}, u32[]{:S(2)}) collective-permute-start(bf16[128,3584]{1,0:T(8,128)(2,1)} %constant_dynamic-slice_fusion.1), channel_id=1, source_target_pairs={{0,4},{12,8},{1,5},{13,9},{2,6},{14,10},{3,7},{15,11},{16,20},{28,... | collective-permute-start | bytes 2752520 | tf_op jit(solution)/shard_map/ppermute | solution.py:122
  92.2 15.4 %collective-permute-done.5 = bf16[128,3584]{1,0:T(8,128)(2,1)} collective-permute-done((bf16[128,3584]{1,0:T(8,128)(2,1)}, bf16[128,3584]{1,0:T(8,128)(2,1)}, u32[]{:S(2)}, u32[]{:S(2)}) %collective-permute-start.5) | collective-permute-done | bytes 917536 | tf_op jit(solution)/shard_map/ppermute | solution.py:122
  115.7 4.2 %collective-permute-start.8 = (bf16[256,3584]{1,0:T(8,128)(2,1)S(1)}, bf16[256,3584]{1,0:T(8,128)(2,1)}, u32[]{:S(2)}, u32[]{:S(2)}) collective-permute-start(bf16[256,3584]{1,0:T(8,128)(2,1)S(1)} %copy-done.3), channel_id=1, source_target_pairs={{0,4},{12,8},{1,5},{13,9},{2,6},{14,10},{3,7},{15,11},{16,20},{28,... | collective-permute-start | bytes 5505032 | tf_op jit(solution)/shard_map/ppermute | solution.py:122
  125.1 14.4 %collective-permute-done.9 = bf16[128,3584]{1,0:T(8,128)(2,1)} collective-permute-done((bf16[128,3584]{1,0:T(8,128)(2,1)}, bf16[128,3584]{1,0:T(8,128)(2,1)}, u32[]{:S(2)}, u32[]{:S(2)}) %collective-permute-start.9) | collective-permute-done | bytes 917536 | tf_op jit(solution)/shard_map/ppermute | solution.py:97
  139.5 15.8 %collective-permute-done.8 = bf16[256,3584]{1,0:T(8,128)(2,1)} collective-permute-done((bf16[256,3584]{1,0:T(8,128)(2,1)S(1)}, bf16[256,3584]{1,0:T(8,128)(2,1)}, u32[]{:S(2)}, u32[]{:S(2)}) %collective-permute-start.8) | collective-permute-done | bytes 1835040 | tf_op jit(solution)/shard_map/ppermute | solution.py:122
  161.4 7.0 %convolution_convert_fusion.9 = bf16[640,512]{1,0:T(8,128)(2,1)} fusion(bf16[640,3584]{1,0:T(8,128)(2,1)} %constant_dynamic-update-slice_fusion, bf16[3584,512]{1,0:T(8,128)(2,1)} %all-gather.11.cloned.1.call-done), kind=kOutput, calls=%fused_computation.68 | convolution fusion | flops 2349137920 | bytes 8912896 | tf_op jit(solution)/shard_map/dot_general | solution.py:13
  174.1 3.4 convolution_convert_fusion.8
  181.2 5.2 %fusion.24 = bf16[480,512]{1,0:T(8,128)(2,1)S(1)} fusion(bf16[512,3584]{1,0:T(8,128)(2,1)} %all-gather.7.cloned.1.call-done, bf16[160,3584]{1,0:T(8,128)(2,1)} %convolution_convert_fusion.1, bf16[160,3584]{1,0:T(8,128)(2,1)} %convolution_convert_fusion.4, bf16[160,3584]{1,0:T(8,128)(2,1)} %copy-done.24), kind=kOutput, calls=%fused_computation.71 | convolution fusion | flops 1772175360 | bytes 7602176 | tf_op jit(solution)/shard_map/dot_general | solution.py:13
  188.4 5.2 %fusion.25 = bf16[480,512]{1,0:T(8,128)(2,1)S(1)} fusion(bf16[512,3584]{1,0:T(8,128)(2,1)} %all-gather.9.cloned.1.call-done, bf16[160,3584]{1,0:T(8,128)(2,1)} %convolution_convert_fusion.1, bf16[160,3584]{1,0:T(8,128)(2,1)} %convolution_convert_fusion.4, bf16[160,3584]{1,0:T(8,128)(2,1)} %copy-done.24), kind=kOutput, calls=%fused_computation.72 | convolution fusion | flops 1772175360 | bytes 7602176 | tf_op jit(solution)/shard_map/dot_general | solution.py:13
  201.0 23.2 %collective-permute-done.12 = bf16[160,1024]{1,0:T(8,128)(2,1)S(1)} collective-permute-done((bf16[160,1024]{1,0:T(8,128)(2,1)S(1)}, bf16[160,1024]{1,0:T(8,128)(2,1)S(1)}, u32[]{:S(2)}, u32[]{:S(2)}) %collective-permute-start.12) | collective-permute-done | bytes 327712 | tf_op jit(solution)/shard_map/ppermute | solution.py:97
  250.6 4.6 %fusion.30 = f32[512,3584]{1,0:T(8,128)S(1)} fusion(bf16[160,3584]{1,0:T(8,128)(2,1)S(1)} %collective-permute-done.11, bf16[160,3584]{1,0:T(8,128)(2,1)} %convolution_convert_fusion.1, bf16[160,3584]{1,0:T(8,128)(2,1)S(1)} %copy-done.13, bf16[160,3584]{1,0:T(8,128)(2,1)} %copy-done.24, bf16[640,1024]{1,0:T(8,128)(2,1)S(1)} %get-tuple-element.55), kind=kOutput, calls=%fused_computation.84 | convolution fusion | flops 2367160320 | bytes 12582912 | tf_op jit(solution)/shard_map/dot_general | solution.py:13
  264.0 5.1 %fusion.37 = f32[3584,512]{1,0:T(8,128)S(1)} fusion(bf16[640,3584]{1,0:T(8,128)(2,1)} %constant_dynamic-update-slice_fusion, bf16[640,1024]{1,0:T(8,128)(2,1)S(1)} %get-tuple-element.56), kind=kOutput, calls=%fused_computation.89 | convolution fusion | flops 2348810240 | bytes 12582912 | tf_op jit(solution)/shard_map/dot_general | solution.py:13
  276.8 3.5 add_convert_fusion.1
  281.8 47.2 %collective-permute-done.18 = bf16[256,3584]{1,0:T(8,128)(2,1)S(1)} collective-permute-done((bf16[256,3584]{1,0:T(8,128)(2,1)}, bf16[256,3584]{1,0:T(8,128)(2,1)S(1)}, u32[]{:S(2)}, u32[]{:S(2)}) %collective-permute-start.18) | collective-permute-done | bytes 1835040 | tf_op jit(solution)/shard_map/ppermute | solution.py:122
  332.2 5.5 %fusion.13 = (f32[3584]{0:T(1024)S(1)}, f32[256]{0:T(256)S(1)}, f32[256]{0:T(256)S(1)}, f32[3584]{0:T(1024)S(1)}, bf16[256,3584]{1,0:T(8,128)(2,1)}) fusion(bf16[256,3584]{1,0:T(8,128)(2,1)S(1)} %copy-done.4, f32[256]{0:T(256)S(1)} %get-tuple-element.72, f32[3584]{0:T(1024)S(1)} %copy-done.21, f32[256]{0:T(256)S(1)} %bitcast.71, ...), kind=kOutput, calls=%fused_computation.39 | convolution fusion | flops 310149632 | bytes 12205056 | tf_op jit(solution)/shard_map/dot_general | solution.py:13
  338.1 3.5 fusion.21
  343.8 24.5 %collective-permute-done.24 = bf16[3584,256]{1,0:T(8,128)(2,1)S(1)} collective-permute-done((bf16[3584,256]{1,0:T(8,128)(2,1)}, bf16[3584,256]{1,0:T(8,128)(2,1)S(1)}, u32[]{:S(2)}, u32[]{:S(2)}) %collective-permute-start.24) | collective-permute-done | bytes 1835040 | tf_op jit(solution)/shard_map/ppermute | solution.py:122
  371.7 35.6 %collective-permute-done.21 = f32[256]{0:T(256)S(1)} collective-permute-done((f32[256]{0:T(256)S(1)}, f32[256]{0:T(256)S(1)}, u32[]{:S(2)}, u32[]{:S(2)}) %collective-permute-start.21) | collective-permute-done | bytes 1056 | tf_op jit(solution)/shard_map/ppermute | solution.py:122
  (202 shorter events, 124.1 us)
Async XLA Ops:
  7.2 148.2 %all-gather.5.cloned.1.call-start = ((), (), s32[]{:S(2)}) async-start(), calls=%async_computation | async-start | bytes 5505024 | tf_op jit(solution)/shard_map/all_gather | solution.py:181
  7.2 44.6 %collective-permute-start = (bf16[256,3584]{1,0:T(8,128)(2,1)}, bf16[256,3584]{1,0:T(8,128)(2,1)}, u32[]{:S(2)}, u32[]{:S(2)}) collective-permute-start(bf16[256,3584]{1,0:T(8,128)(2,1)} %param.7), channel_id=1, source_target_pairs={{0,4},{12,8},{1,5},{13,9},{2,6},{14,10},{3,7},{15,11},{16,20},{28,... | collective-permute-start | bytes 5505032 | tf_op jit(solution)/shard_map/ppermute | solution.py:122
  52.6 26.7 %collective-permute-start.4 = (bf16[160,3584]{1,0:T(8,128)(2,1)S(1)}, bf16[160,3584]{1,0:T(8,128)(2,1)S(1)}, u32[]{:S(2)}, u32[]{:S(2)}) collective-permute-start(bf16[160,3584]{1,0:T(8,128)(2,1)S(1)} %convolution_convert_fusion.6), channel_id=1, source_target_pairs={{4,8},{8,4},{5,9},{9,5},{6,10},{10,6},{7,11},{11,7},{20,24},{24,20... | collective-permute-start | bytes 3440648 | tf_op jit(solution)/shard_map/ppermute | solution.py:122
  53.4 25.9 %collective-permute-start.3 = (bf16[1792,256]{1,0:T(8,128)(2,1)}, bf16[1792,256]{1,0:T(8,128)(2,1)}, u32[]{:S(2)}, u32[]{:S(2)}) collective-permute-start(bf16[1792,256]{1,0:T(8,128)(2,1)} %constant_dynamic-slice_fusion), channel_id=1, source_target_pairs={{0,4},{12,8},{1,5},{13,9},{2,6},{14,10},{3,7},{15,11},{16,20},{28,... | collective-permute-start | bytes 2752520 | tf_op jit(solution)/shard_map/ppermute | solution.py:122
  80.4 30.3 %collective-permute-start.6 = (bf16[160,3584]{1,0:T(8,128)(2,1)}, bf16[160,3584]{1,0:T(8,128)(2,1)S(1)}, u32[]{:S(2)}, u32[]{:S(2)}) collective-permute-start(bf16[160,3584]{1,0:T(8,128)(2,1)} %convolution_convert_fusion.3), channel_id=1, source_target_pairs={{4,8},{8,4},{5,9},{9,5},{6,10},{10,6},{7,11},{11,7},{20,24},{24,20... | collective-permute-start | bytes 3440648 | tf_op jit(solution)/shard_map/ppermute | solution.py:122
  81.1 26.4 %collective-permute-start.5 = (bf16[128,3584]{1,0:T(8,128)(2,1)}, bf16[128,3584]{1,0:T(8,128)(2,1)}, u32[]{:S(2)}, u32[]{:S(2)}) collective-permute-start(bf16[128,3584]{1,0:T(8,128)(2,1)} %constant_dynamic-slice_fusion.1), channel_id=1, source_target_pairs={{0,4},{12,8},{1,5},{13,9},{2,6},{14,10},{3,7},{15,11},{16,20},{28,... | collective-permute-start | bytes 2752520 | tf_op jit(solution)/shard_map/ppermute | solution.py:122
  114.1 47.3 %all-gather.11.cloned.1.call-start = ((), (), s32[]{:S(2)}) async-start(), calls=%async_computation.3 | async-start | bytes 5505024 | tf_op jit(solution)/shard_map/all_gather | solution.py:129
  114.9 66.3 %all-gather.7.cloned.1.call-start = ((), (), s32[]{:S(2)}) async-start(), calls=%async_computation.1 | async-start | bytes 5505024 | tf_op jit(solution)/shard_map/all_gather | solution.py:130
  115.6 72.8 %all-gather.9.cloned.1.call-start = ((), (), s32[]{:S(2)}) async-start(), calls=%async_computation.2 | async-start | bytes 5505024 | tf_op jit(solution)/shard_map/all_gather | solution.py:183
  115.7 39.7 %collective-permute-start.8 = (bf16[256,3584]{1,0:T(8,128)(2,1)S(1)}, bf16[256,3584]{1,0:T(8,128)(2,1)}, u32[]{:S(2)}, u32[]{:S(2)}) collective-permute-start(bf16[256,3584]{1,0:T(8,128)(2,1)S(1)} %copy-done.3), channel_id=1, source_target_pairs={{0,4},{12,8},{1,5},{13,9},{2,6},{14,10},{3,7},{15,11},{16,20},{28,... | collective-permute-start | bytes 5505032 | tf_op jit(solution)/shard_map/ppermute | solution.py:122
  168.4 28.9 %collective-permute-start.13 = (bf16[640,512]{1,0:T(8,128)(2,1)}, bf16[640,512]{1,0:T(8,128)(2,1)}, u32[]{:S(2)}, u32[]{:S(2)}) collective-permute-start(bf16[640,512]{1,0:T(8,128)(2,1)} %convolution_convert_fusion.9), channel_id=1, source_target_pairs={{0,2},{2,0},{1,3},{3,1},{4,6},{6,4},{5,7},{7,5},{8,10},{10,8},{9,1... | collective-permute-start | bytes 1966088 | tf_op jit(solution)/shard_map/ppermute | solution.py:97
  193.8 30.5 %collective-permute-start.10 = (bf16[480,1024]{1,0:T(8,128)(2,1)S(1)}, bf16[480,1024]{1,0:T(8,128)(2,1)S(1)}, u32[]{:S(2)}, u32[]{:S(2)}) collective-permute-start(bf16[480,1024]{1,0:T(8,128)(2,1)S(1)} %pad_maximum_fusion.11), channel_id=1, source_target_pairs={{0,2},{2,0},{1,3},{3,1},{4,6},{6,4},{5,7},{7,5},{8,10},{10,8},{9,1... | collective-permute-start | bytes 2949128 | tf_op jit(solution)/shard_map/ppermute | solution.py:97
  196.7 27.5 %collective-permute-start.12 = (bf16[160,1024]{1,0:T(8,128)(2,1)S(1)}, bf16[160,1024]{1,0:T(8,128)(2,1)S(1)}, u32[]{:S(2)}, u32[]{:S(2)}) collective-permute-start(bf16[160,1024]{1,0:T(8,128)(2,1)S(1)} %pad_maximum_fusion.14), channel_id=1, source_target_pairs={{0,2},{2,0},{1,3},{3,1},{4,6},{6,4},{5,7},{7,5},{8,10},{10,8},{9,1... | collective-permute-start | bytes 983048 | tf_op jit(solution)/shard_map/ppermute | solution.py:97
  231.3 37.9 %collective-permute-start.17 = (bf16[256,3584]{1,0:T(8,128)(2,1)}, bf16[256,3584]{1,0:T(8,128)(2,1)}, u32[]{:S(2)}, u32[]{:S(2)}) collective-permute-start(bf16[256,3584]{1,0:T(8,128)(2,1)} %dynamic-slice_convert_fusion.3), channel_id=1, source_target_pairs={{0,1},{1,0},{2,3},{3,2},{4,5},{5,4},{6,7},{7,6},{8,9},{9,8},{10,11... | collective-permute-start | bytes 5505032 | tf_op jit(solution)/shard_map/ppermute | solution.py:97
  243.6 36.7 %collective-permute-start.16 = (bf16[160,3584]{1,0:T(8,128)(2,1)}, bf16[160,3584]{1,0:T(8,128)(2,1)}, u32[]{:S(2)}, u32[]{:S(2)}) collective-permute-start(bf16[160,3584]{1,0:T(8,128)(2,1)} %fusion.4), channel_id=1, source_target_pairs={{4,8},{8,4},{5,9},{9,5},{6,10},{10,6},{7,11},{11,7},{20,24},{24,20... | collective-permute-start | bytes 3440648 | tf_op jit(solution)/shard_map/ppermute | solution.py:122
  248.9 32.9 %collective-permute-start.15 = (bf16[160,3584]{1,0:T(8,128)(2,1)}, bf16[160,3584]{1,0:T(8,128)(2,1)}, u32[]{:S(2)}, u32[]{:S(2)}) collective-permute-start(bf16[160,3584]{1,0:T(8,128)(2,1)} %fusion.3), channel_id=1, source_target_pairs={{4,8},{8,4},{5,9},{9,5},{6,10},{10,6},{7,11},{11,7},{20,24},{24,20... | collective-permute-start | bytes 3440648 | tf_op jit(solution)/shard_map/ppermute | solution.py:122
  256.7 81.1 %collective-permute-start.25 = (bf16[256,3584]{1,0:T(8,128)(2,1)}, bf16[256,3584]{1,0:T(8,128)(2,1)}, u32[]{:S(2)}, u32[]{:S(2)}) collective-permute-start(bf16[256,3584]{1,0:T(8,128)(2,1)} %dynamic-slice_convert_fusion), channel_id=1, source_target_pairs={{0,1},{1,0},{2,3},{3,2},{4,5},{5,4},{6,7},{7,6},{8,9},{9,8},{10,11... | collective-permute-start | bytes 5505032 | tf_op jit(solution)/shard_map/ppermute | solution.py:97
  272.6 56.4 %collective-permute-start.18 = (bf16[256,3584]{1,0:T(8,128)(2,1)}, bf16[256,3584]{1,0:T(8,128)(2,1)S(1)}, u32[]{:S(2)}, u32[]{:S(2)}) collective-permute-start(bf16[256,3584]{1,0:T(8,128)(2,1)} %add_convert_fusion.3), channel_id=1, source_target_pairs={{4,0},{8,12},{5,1},{9,13},{6,2},{10,14},{7,3},{11,15},{20,16},{24,... | collective-permute-start | bytes 5505032 | tf_op jit(solution)/shard_map/ppermute | solution.py:122
  276.7 67.2 %collective-permute-start.22 = (bf16[3584,256]{1,0:T(8,128)(2,1)}, bf16[3584,256]{1,0:T(8,128)(2,1)S(1)}, u32[]{:S(2)}, u32[]{:S(2)}) collective-permute-start(bf16[3584,256]{1,0:T(8,128)(2,1)} %dynamic-slice_convert_fusion.2), channel_id=1, source_target_pairs={{0,1},{1,0},{2,3},{3,2},{4,5},{5,4},{6,7},{7,6},{8,9},{9,8},{10,11... | collective-permute-start | bytes 5505032 | tf_op jit(solution)/shard_map/ppermute | solution.py:97
  280.2 88.0 %collective-permute-start.24 = (bf16[3584,256]{1,0:T(8,128)(2,1)}, bf16[3584,256]{1,0:T(8,128)(2,1)S(1)}, u32[]{:S(2)}, u32[]{:S(2)}) collective-permute-start(bf16[3584,256]{1,0:T(8,128)(2,1)} %add_convert_fusion.1), channel_id=1, source_target_pairs={{4,0},{8,12},{5,1},{9,13},{6,2},{10,14},{7,3},{11,15},{20,16},{24,... | collective-permute-start | bytes 5505032 | tf_op jit(solution)/shard_map/ppermute | solution.py:122
  330.9 77.1 %collective-permute-start.19 = (bf16[256,3584]{1,0:T(8,128)(2,1)S(1)}, bf16[256,3584]{1,0:T(8,128)(2,1)S(1)}, u32[]{:S(2)}, u32[]{:S(2)}) collective-permute-start(bf16[256,3584]{1,0:T(8,128)(2,1)S(1)} %fusion.2), channel_id=1, source_target_pairs={{4,0},{8,12},{5,1},{9,13},{6,2},{10,14},{7,3},{11,15},{20,16},{24,... | collective-permute-start | bytes 5505032 | tf_op jit(solution)/shard_map/ppermute | solution.py:122
  341.7 65.5 %collective-permute-start.21 = (f32[256]{0:T(256)S(1)}, f32[256]{0:T(256)S(1)}, u32[]{:S(2)}, u32[]{:S(2)}) collective-permute-start(f32[256]{0:T(256)S(1)} %bitcast.72), channel_id=1, source_target_pairs={{4,0},{8,12},{5,1},{9,13},{6,2},{10,14},{7,3},{11,15},{20,16},{24,... | collective-permute-start | bytes 3080 | tf_op jit(solution)/shard_map/ppermute | solution.py:122
  343.0 27.3 %collective-permute-start.27 = (f32[3584]{0:T(1024)S(1)}, f32[3584]{0:T(1024)S(1)}, u32[]{:S(2)}, u32[]{:S(2)}) collective-permute-start(f32[3584]{0:T(1024)S(1)} %add.143), channel_id=1, source_target_pairs={{4,8},{8,4},{5,9},{9,5},{6,10},{10,6},{7,11},{11,7},{20,24},{24,20... | collective-permute-start | bytes 43016 | tf_op jit(solution)/shard_map/ppermute | solution.py:122
  370.4 37.0 %collective-permute-start.28 = (f32[3584]{0:T(1024)S(1)}, f32[3584]{0:T(1024)S(1)}, u32[]{:S(2)}, u32[]{:S(2)}) collective-permute-start(f32[3584]{0:T(1024)S(1)} %add.144), channel_id=1, source_target_pairs={{4,0},{8,12},{5,1},{9,13},{6,2},{10,14},{7,3},{11,15},{20,16},{24,... | collective-permute-start | bytes 43016 | tf_op jit(solution)/shard_map/ppermute | solution.py:122
  (41 other events, 500.8 us)
Sparse Core Ops, SparseCore 0:
  114.2 11.8 all-gather.4
  127.7 13.5 all-gather.10
  142.8 14.0 all-gather.6
  158.9 14.0 all-gather.8
